TPU v7x, 32 devices: a whole 2x2x4 slice. The times are simulated.
32 devices in a mesh: ex: 8 (over z, core), hid: 4 (over y, x).
Axes of the slice: x: 2, y: 2, z: 4, core: 2. Of those that a mesh axis runs over, the one named last changes fastest.
Arguments:
- tokens: bfloat16 [512, 2048], P(('ex', 'hid')), may hold values from -6 to 6
- cotangent: bfloat16 [512, 2048], P(('ex', 'hid')), may hold values from -6 to 6
- gates: float32 [512, 4], P(('ex', 'hid')), may hold values from 0.1 to 1
- routes: int32 [512, 4], P(('ex', 'hid')), may hold values from 0 to 15, all different within a row; in each aligned block of 16 rows (0 to 15, 16 to 31, ...) at most 8 rows name the same one
- w_gate: bfloat16 [32, 704, 2048], P(('ex', 'hid')), may hold values from -0.125 to 0.125
- w_up: bfloat16 [32, 704, 2048], P(('ex', 'hid')), may hold values from -0.125 to 0.125
- w_down: bfloat16 [32, 704, 2048], P(('ex', 'hid')), may hold values from -0.15625 to 0.15625
Outputs:
- grad_tokens: bfloat16 [512, 2048], P(('ex', 'hid'))
Inputs may be any that keep to these rules, and one draw needn't show every extreme that they name: `routes`: among the 16 tokens of one device (aligned blocks of rows) no expert is named more than 8 times, a bound that some block reaches; a token's 4 experts differ.
All inputs are finite; a program needn't handle non-finite values.
Results may differ from a plain program's by a relative error of at most 0.007.
Values may be sent and summed in bfloat16 or wider, within the bound.
A program may use at most 64 MiB of HBM per device.

v0:
```python
import jax
import jax.numpy as jnp
from jax import lax
from jax.sharding import PartitionSpec as P

EXP_DEV = 2


def hidden_grad(inputs, cotan, wgate, wup, wdown):
    dims = (((1,), (1,)), ((), ()))
    gate = lax.dot_general(inputs, wgate, dims, preferred_element_type=jnp.float32)
    upper = lax.dot_general(inputs, wup, dims, preferred_element_type=jnp.float32)
    hidden = lax.dot_general(cotan, wdown, dims, preferred_element_type=jnp.float32)
    sig = jax.nn.sigmoid(gate)
    d_up = (hidden * gate * sig).astype(jnp.bfloat16)
    d_gate = (hidden * upper * sig * (1.0 + gate * (1.0 - sig))).astype(jnp.bfloat16)
    first = jnp.dot(d_gate, wgate, preferred_element_type=jnp.float32)
    second = jnp.dot(d_up, wup, preferred_element_type=jnp.float32)
    return first + second


def per_device(tokens, cotangent, gates, routes, w_gate, w_up, w_down):
    n_ex = lax.axis_size("ex")
    n_hid = lax.axis_size("hid")
    tok_dev, width = tokens.shape
    top = routes.shape[1]
    experts_all = EXP_DEV * n_ex
    blocks = n_hid // EXP_DEV
    slot_cap = max(2, (2 * tok_dev * top + experts_all - 1) // experts_all)
    flat = routes.reshape(-1)
    count = flat.shape[0]
    order = jnp.arange(count, dtype=jnp.int32)
    same = flat[:, None] == flat[None, :]
    earlier = order[None, :] < order[:, None]
    slot = jnp.sum(jnp.where(same & earlier, 1, 0), axis=1).astype(jnp.int32)
    owner_ex = flat // EXP_DEV
    local = flat % EXP_DEV
    rows_x = jnp.repeat(tokens, top, axis=0)
    rows_dy = jnp.repeat(cotangent, top, axis=0).astype(jnp.float32)
    scaled = (gates.reshape(-1)[:, None] * rows_dy).astype(jnp.bfloat16)
    stacked = jnp.stack([rows_x, scaled], axis=1)
    buffer = (
        jnp.zeros((EXP_DEV, 2, n_ex, slot_cap, width), jnp.bfloat16)
        .at[local, :, owner_ex, slot]
        .set(stacked)
    )
    arrived = lax.all_to_all(buffer, "ex", split_axis=2, concat_axis=2, tiled=True)
    tail = arrived.shape[1:]
    received = lax.all_to_all(
        jnp.broadcast_to(arrived[:, None], (EXP_DEV, blocks) + tail).reshape((n_hid,) + tail),
        "hid",
        split_axis=0,
        concat_axis=0,
        tiled=True,
    )
    rows = n_hid * n_ex * slot_cap
    inputs = received[:, 0].reshape(rows, width)
    cotan = received[:, 1].reshape(rows, width)
    partial_value = hidden_grad(inputs, cotan, w_gate[0], w_up[0], w_down[0]).astype(jnp.bfloat16)
    partial_value = partial_value.reshape(n_hid, n_ex, slot_cap, width)
    moved = lax.all_to_all(partial_value, "ex", split_axis=1, concat_axis=1, tiled=True)
    landed = lax.all_to_all(moved, "hid", split_axis=0, concat_axis=0, tiled=True)
    back = jnp.sum(
        landed.astype(jnp.float32).reshape(EXP_DEV, blocks, n_ex, slot_cap, width), axis=1
    ).astype(jnp.bfloat16)
    index = (local * n_ex + owner_ex) * slot_cap + slot
    picked = back.reshape(-1, width)[index].reshape(tok_dev, top, width).astype(jnp.float32)
    return jnp.sum(picked, axis=1).astype(jnp.bfloat16)


def solution(mesh):
    in_specs = (
        P(("ex", "hid"), None),
        P(("ex", "hid"), None),
        P(("ex", "hid"), None),
        P(("ex", "hid"), None),
        P(("ex", "hid"), None, None),
        P(("ex", "hid"), None, None),
        P(("ex", "hid"), None, None),
    )
    out_specs = P(("ex", "hid"), None)
    return jax.shard_map(
        per_device, mesh=mesh, in_specs=in_specs, out_specs=out_specs, check_vma=False
    )
```

profile of v0, /device:TPU:0, one launch (start us, length us, event | category | flops | bytes accessed | tf_op | source)
XLA Modules:
  0.0 155.1 jit_solution(10778613472214240220)
XLA Ops:
  1.3 1.7 %broadcast_in_dim.33 = f32[16,4,2048]{2,1,0:T(4,128)} broadcast(bf16[16,2048]{1,0:T(8,128)(2,1)} %param.8), dimensions={0,2} | broadcast | bytes 589824 | tf_op jit(solution)/shard_map/broadcast_in_dim | solution.py:39
  3.0 1.2 convert_element_type.44
  5.1 1.6 %broadcast_in_dim.32 = bf16[16,4,2048]{2,1,0:T(4,128)(2,1)} broadcast(bf16[16,2048]{1,0:T(8,128)(2,1)} %param.7), dimensions={0,2} | broadcast | bytes 327680 | tf_op jit(solution)/shard_map/broadcast_in_dim | solution.py:38
  6.7 1.7 %stack_reshape.3 = bf16[64,1,2048]{2,0,1:T(8,128)(2,1)} reshape(bf16[16,4,2048]{2,1,0:T(4,128)(2,1)} %broadcast_in_dim.32) | data formatting | bytes 524288 | tf_op jit(solution)/shard_map/stack;reshape | solution.py:41
  8.5 1.0 pad_maximum_fusion
  10.1 1.8 %broadcast_in_dim.16 = bf16[2,2,8,8,2048]{4,1,3,2,0:T(2,128)(2,1)} broadcast(bf16[]{:T(256)} %constant.32.clone.1), dimensions={} | broadcast | bytes 1048578 | tf_op jit(solution)/shard_map/broadcast_in_dim | solution.py:43
  11.9 9.3 %scatter_fusion = bf16[2,2,8,8,2048]{4,1,3,2,0:T(2,128)(2,1)} fusion(bf16[2,2,8,8,2048]{4,1,3,2,0:T(2,128)(2,1)} %broadcast_in_dim.16, s32[64]{0:T(128)S(1)} %fusion.39, bf16[64,2,2048]{2,1,0:T(2,128)(2,1)S(1)} %copy.37), kind=kCustom, calls=%fused_computation.1 | custom fusion | bytes 1573632 | tf_op jit(solution)/shard_map/scatter | solution.py:45
  21.3 2.3 %copy.38 = bf16[2,2,8,8,2048]{4,1,3,0,2:T(2,128)(2,1)S(1)} copy(bf16[2,2,8,8,2048]{4,1,3,2,0:T(2,128)(2,1)} %scatter_fusion) | data formatting | bytes 2097152 | tf_op jit(solution)/shard_map/scatter | solution.py:45
  23.6 32.7 %all_to_all.20 = bf16[2,2,8,8,2048]{4,1,3,0,2:T(2,128)(2,1)S(1)} all-to-all(bf16[2,2,8,8,2048]{4,1,3,0,2:T(2,128)(2,1)S(1)} %copy.38), channel_id=1, replica_groups=mesh['ex'=8,'hid'=4] {'ex'}, dimensions={2} | all-to-all | bytes 2097152 | tf_op jit(solution)/shard_map/all_to_all | solution.py:47
  56.9 28.5 %all_to_all.21 = bf16[4,2,8,8,2048]{4,3,2,1,0:T(8,128)(2,1)S(1)} all-to-all(bf16[4,2,8,8,2048]{4,3,2,1,0:T(8,128)(2,1)S(1)} %bitcast.49), channel_id=1, replica_groups=mesh['ex'=8,'hid'=4] {'hid'}, dimensions={0} | all-to-all | bytes 4194304 | tf_op jit(solution)/shard_map/all_to_all | solution.py:49
  85.6 1.0 copy-done.1
  86.5 1.1 copy-done.3
  87.6 1.8 %fusion.2 = f32[256,704]{0,1:T(8,128)} fusion(bf16[256,2048]{1,0:T(8,128)(2,1)S(1)} %bitcast.51, bf16[1,704,2048]{2,1,0:T(8,128)(2,1)S(1)} %copy-done.3), kind=kOutput, calls=%fused_computation.4 | convolution fusion | flops 738197504 | bytes 4653056 | tf_op jit(solution)/shard_map/dot_general | solution.py:11
  89.4 1.9 %fusion.8 = f32[256,704]{0,1:T(8,128)} fusion(bf16[256,2048]{1,0:T(8,128)(2,1)S(1)} %bitcast.53, bf16[1,704,2048]{2,1,0:T(8,128)(2,1)S(1)} %copy-done.2), kind=kOutput, calls=%fused_computation.10 | convolution fusion | flops 738197504 | bytes 4653056 | tf_op jit(solution)/shard_map/dot_general | solution.py:13
  91.3 7.2 %fusion = f32[256,2048]{1,0:T(8,128)} fusion(bf16[1,704,2048]{2,1,0:T(8,128)(2,1)} %param.11, f32[256,704]{0,1:T(8,128)} %fusion.8, bf16[256,2048]{1,0:T(8,128)(2,1)} %bitcast.52, bf16[1,704,2048]{2,1,0:T(8,128)(2,1)S(1)} %copy-done, f32[256,704]{0,1:T(8,128)} %fusion.2), kind=kOutput, calls=%fused_computation.2 | convolution fusion | flops 1478197248 | bytes 10354688 | tf_op jit(solution)/shard_map/dot_general | solution.py:17
  98.6 3.1 %fusion.13 = bf16[256,2048]{1,0:T(8,128)(2,1)S(1)} fusion(f32[256,2048]{1,0:T(8,128)} %fusion, bf16[1,704,2048]{2,1,0:T(8,128)(2,1)S(1)} %copy-done, f32[256,704]{0,1:T(8,128)} %fusion.8, f32[256,704]{0,1:T(8,128)} %fusion.2), kind=kOutput, calls=%fused_computation.13 | convolution fusion | flops 740327424 | bytes 7471104 | tf_op jit(solution)/shard_map/dot_general | solution.py:18
  101.8 29.5 %all_to_all.22 = bf16[4,8,8,2048]{3,2,0,1:T(8,128)(2,1)S(1)} all-to-all(bf16[4,8,8,2048]{3,2,0,1:T(8,128)(2,1)S(1)} %copy.40), channel_id=1, replica_groups=mesh['ex'=8,'hid'=4] {'ex'}, dimensions={1} | all-to-all | bytes 2097152 | tf_op jit(solution)/shard_map/all_to_all | solution.py:61
  131.3 1.1 copy.41
  132.4 4.2 %all-to-all-start.3 = ((bf16[4,8,8,2048]{3,2,1,0:T(8,128)(2,1)}), bf16[4,8,8,2048]{3,2,1,0:T(8,128)(2,1)}, u32[]{:S(2)}, u32[]{:S(2)}) async-start(bf16[4,8,8,2048]{3,2,1,0:T(8,128)(2,1)} %copy.41), calls=%async_computation.3 | async-start | bytes 2097152 | tf_op jit(solution)/shard_map/all_to_all | solution.py:62
  136.6 13.6 %all-to-all-done.3 = bf16[4,8,8,2048]{3,2,1,0:T(8,128)(2,1)} async-done(((bf16[4,8,8,2048]{3,2,1,0:T(8,128)(2,1)}), bf16[4,8,8,2048]{3,2,1,0:T(8,128)(2,1)}, u32[]{:S(2)}, u32[]{:S(2)}) %all-to-all-start.3) | async-done | bytes 1048608 | tf_op jit(solution)/shard_map/all_to_all | solution.py:62
  150.2 1.4 bitcast_reduce_fusion
  151.6 1.4 gather_fusion
  153.0 1.1 reshape.250
  154.1 0.9 reduce_sum.35
  (21 shorter events, 3.6 us)
Async XLA Ops:
  0.0 91.3 %copy-start = (bf16[1,704,2048]{2,1,0:T(8,128)(2,1)S(1)}, bf16[1,704,2048]{2,1,0:T(8,128)(2,1)}, u32[]{:S(2)}) copy-start(bf16[1,704,2048]{2,1,0:T(8,128)(2,1)} %param.12) | copy-start | bytes 8650756
  85.4 2.2 %copy-start.3 = (bf16[1,704,2048]{2,1,0:T(8,128)(2,1)S(1)}, bf16[1,704,2048]{2,1,0:T(8,128)(2,1)}, u32[]{:S(2)}) copy-start(bf16[1,704,2048]{2,1,0:T(8,128)(2,1)} %param.11) | copy-start | bytes 8650756
  85.6 1.0 copy-start.1
  85.6 3.9 %copy-start.2 = (bf16[1,704,2048]{2,1,0:T(8,128)(2,1)S(1)}, bf16[1,704,2048]{2,1,0:T(8,128)(2,1)}, u32[]{:S(2)}) copy-start(bf16[1,704,2048]{2,1,0:T(8,128)(2,1)} %param.13) | copy-start | bytes 8650756
  132.4 17.9 %all-to-all-start.3 = ((bf16[4,8,8,2048]{3,2,1,0:T(8,128)(2,1)}), bf16[4,8,8,2048]{3,2,1,0:T(8,128)(2,1)}, u32[]{:S(2)}, u32[]{:S(2)}) async-start(bf16[4,8,8,2048]{3,2,1,0:T(8,128)(2,1)} %copy.41), calls=%async_computation.3 | async-start | bytes 2097152 | tf_op jit(solution)/shard_map/all_to_all | solution.py:62
where the time goes:
time: 156 us; the launch traced here: 155 us
  blocking collectives  90.8 us (58%)
  local copies, waits for them, and re-layouts  28.6 us (18%)
  matrix products  14 us (9%)
  waiting for transfers between devices  13.6 us (9%)
  starting transfers between devices  4.23 us (3%)
  other arithmetic  3.65 us (2%)
    all_to_all x1, blocking collectives, per_device(): lax.all_to_all(buffer, 'ex', split_axis=2, concat_axis=2, tiled=True)  32.7 us
    all_to_all x1, blocking collectives, per_device(): lax.all_to_all(partial_value, 'ex', split_axis=1, concat_axis=1, tiled=True)  29.5 us
    all_to_all x1, blocking collectives, per_device(): lax.all_to_all(jnp.broadcast_to(arrived[:, None], (EXP_DEV, blocks) + tai...  28.5 us
    all_to_all x1, waiting for transfers between devices, per_device(): lax.all_to_all(moved, 'hid', split_axis=0, concat_axis=0, tiled=True)  13.6 us
    scatter x2, local copies, waits for them, and re-layouts, per_device(): buffer = jnp.zeros((EXP_DEV, 2, n_ex, slot_cap, width), jnp.bfloat16).at[...  11.6 us
    dot_general x1, matrix products, hidden_grad(): first = jnp.dot(d_gate, wgate, preferred_element_type=jnp.float32)  7.25 us
    all_to_all x1, starting transfers between devices, per_device(): lax.all_to_all(moved, 'hid', split_axis=0, concat_axis=0, tiled=True)  4.23 us
    unnamed x10, local copies, waits for them, and re-layouts  3.71 us
  transfers between devices with their start and end apart: 1, of which 1 were waited for; matrix products, arithmetic and copies ran while one was open for 0% of the time, Pallas kernels for 0%

commit v1 on v0

--- a/solution.py
+++ b/solution.py
@@ -1,9 +1,259 @@
+import functools
+
 import jax
 import jax.numpy as jnp
 from jax import lax
+from jax.experimental import pallas as pl
+from jax.experimental.pallas import tpu as pltpu
 from jax.sharding import PartitionSpec as P
 
 EXP_DEV = 2
+CORES = 2
+LANES = 128
+F32 = jnp.float32
+BF16 = jnp.bfloat16
+
+
+def dense_kernel(
+    blocks, tok_ref, cot_ref, gates_ref, routes_ref, wg_hbm, wu_hbm, wd_hbm, out_ref,
+    rows, wg, wu, wd, ys, dgs, dus, part, from_sib, pair, from_x, from_y, half_x, half_y,
+    from_y2, from_x2, plane, from_z, w_sem, send_sem, recv_sem,
+):
+    tok_dev, width = tok_ref.shape
+    top = gates_ref.shape[1]
+    half = width // 2
+    ex, hid = lax.axis_index("ex"), lax.axis_index("hid")
+    z, c = ex // CORES, ex % CORES
+    y, x = hid // 2, hid % 2
+    expert = (ex * lax.axis_size("hid") + hid) // blocks
+    experts = EXP_DEV * lax.axis_size("ex")
+
+    loads = [
+        pltpu.make_async_copy(src.at[0], dst, w_sem.at[i])
+        for i, (src, dst) in enumerate(((wg_hbm, wg), (wu_hbm, wu), (wd_hbm, wd)))
+    ]
+    for load in loads:
+        load.start()
+
+    def device(zz, cc, yy, xx):
+        return (zz * CORES + cc, yy * 2 + xx)
+
+    z_of = (z, z + 1 - 2 * (z % 2), (z + 2) % 4, 3 - z)
+    at_x = device(z, c, y, 1 - x)
+    at_y = device(z, c, 1 - y, x)
+    sibling = device(z, 1 - c, y, x)
+    at_z = [device(zz, c, y, x) for zz in z_of]
+    partners = [at_x, at_y, sibling] + at_z[1:]
+    barrier = pltpu.get_barrier_semaphore()
+    for partner in partners:
+        pl.semaphore_signal(barrier, inc=1, device_id=partner, device_id_type=pl.DeviceIdType.MESH)
+
+    lane = lax.broadcasted_iota(jnp.int32, (tok_dev, LANES), 1)
+    dense = jnp.zeros((tok_dev, LANES), F32)
+    for k in range(top):
+        dense += jnp.where(lane % experts == routes_ref[:, k : k + 1], gates_ref[:, k : k + 1], 0.0)
+    high = dense.astype(BF16).astype(F32)
+    rest = dense - high
+    mid = rest.astype(BF16).astype(F32)
+    low = rest - mid
+    term = lane // experts
+    terms = jnp.where(term == 0, high, jnp.where(term == 1, mid, jnp.where(term == 2, low, 0.0)))
+    rows[0, 0, 0, :tok_dev, :width] = tok_ref[...]
+    rows[0, 0, 0, :tok_dev, width:] = terms.astype(BF16)
+    rows[0, 0, 0, tok_dev:, :width] = cot_ref[...]
+    rows[0, 0, 0, tok_dev:, width:] = jnp.zeros((tok_dev, LANES), BF16)
+    pl.semaphore_wait(barrier, len(partners))
+
+    copies = []
+
+    def send(src, dst, target):
+        k = len(copies)
+        copy = pltpu.make_async_remote_copy(
+            src_ref=src, dst_ref=dst, send_sem=send_sem.at[k], recv_sem=recv_sem.at[k],
+            device_id=target, device_id_type=pl.DeviceIdType.MESH,
+        )
+        copy.start()
+        copies.append(copy)
+        return copy
+
+    along_z, along_x, along_y, diag_x, diag_y, cross = [None] * 4, [None] * 4, [None] * 4, [None] * 4, [None] * 4, {}
+
+    def spread(i):
+        along_x[i] = send(rows.at[i, 0, 0], rows.at[i, 0, 1], at_x)
+        along_y[i] = send(rows.at[i, 0, 0], rows.at[i, 0, 2], at_y)
+        cross[i, 0] = send(rows.at[i, 0, 0], rows.at[i, 1, 0], sibling)
+
+    def relay(i):
+        along_x[i].wait_recv()
+        diag_y[i] = send(rows.at[i, 0, 1, pl.ds(0, tok_dev)], rows.at[i, 0, 3, pl.ds(0, tok_dev)], at_y)
+        cross[i, 1] = send(rows.at[i, 0, 1], rows.at[i, 1, 1], sibling)
+        along_y[i].wait_recv()
+        diag_x[i] = send(
+            rows.at[i, 0, 2, pl.ds(tok_dev, tok_dev)], rows.at[i, 0, 3, pl.ds(tok_dev, tok_dev)], at_x
+        )
+        cross[i, 2] = send(rows.at[i, 0, 2], rows.at[i, 1, 2], sibling)
+
+    def close(i):
+        diag_y[i].wait_recv()
+        diag_x[i].wait_recv()
+        cross[i, 3] = send(rows.at[i, 0, 3], rows.at[i, 1, 3], sibling)
+
+    def arrived(i):
+        for r in range(4):
+            cross[i, r].wait_recv()
+
+    def expand(i):
+        count = 2 * CORES * 4 * tok_dev
+        gate_rows = rows[pl.ds(i, 2), :, :, pl.ds(0, tok_dev), pl.ds(width, LANES)].reshape(count, LANES)
+        lanes = lax.broadcasted_iota(jnp.int32, (count, LANES), 1)
+        mine = (lanes % experts == expert) & (lanes < 3 * experts)
+        gate = jnp.sum(jnp.where(mine, gate_rows.astype(F32), 0.0), axis=1, keepdims=True)
+        cot = rows[pl.ds(i, 2), :, :, pl.ds(tok_dev, tok_dev), pl.ds(0, width)].reshape(count, width)
+        ys[...] = (gate * cot.astype(F32)).astype(BF16)
+
+    def hidden(i):
+        count = 2 * CORES * 4 * tok_dev
+        dims = (((1,), (1,)), ((), ()))
+        inputs = rows[pl.ds(i, 2), :, :, pl.ds(0, tok_dev), pl.ds(0, width)].reshape(count, width)
+        gate = lax.dot_general(inputs, wg[...], dims, preferred_element_type=F32)
+        upper = lax.dot_general(inputs, wu[...], dims, preferred_element_type=F32)
+        down = lax.dot_general(ys[...], wd[...], dims, preferred_element_type=F32)
+        sig = jax.nn.sigmoid(gate)
+        dus[...] = (down * gate * sig).astype(BF16)
+        dgs[...] = (down * upper * sig * (1.0 + gate * (1.0 - sig))).astype(BF16)
+
+    def back(i):
+        step = width // 4
+
+        def body(n, carry):
+            at = pl.ds(pl.multiple_of(n * step, step), step)
+            value = jnp.dot(dgs[...], wg[:, at], preferred_element_type=F32)
+            value += jnp.dot(dus[...], wu[:, at], preferred_element_type=F32)
+            part[pl.ds(i, 2), :, :, :, at] = value.astype(BF16).reshape(2, CORES, 4, tok_dev, step)
+            return carry
+
+        lax.fori_loop(0, 4, body, 0)
+
+    sib, first_x, first_y, second_x, second_y, home = {}, {}, {}, {}, {}, {}
+
+    def reduce_sibling(i):
+        sib[i] = send(part.at[i, 1], from_sib.at[i], sibling)
+
+    def reduce_first(i):
+        sib[i].wait_recv()
+        total = part[i, 0].astype(F32) + from_sib[i].astype(F32)
+        pair[i] = total.astype(BF16).reshape(2, 2, tok_dev, width)
+        first_x[i] = send(pair.at[i, :, 1, :, pl.ds(0, half)], from_x.at[i], at_x)
+        first_y[i] = send(pair.at[i, 1, :, :, pl.ds(half, half)], from_y.at[i], at_y)
+
+    def reduce_second(i):
+        first_x[i].wait_recv()
+        half_x[i] = (pair[i, :, 0, :, :half].astype(F32) + from_x[i].astype(F32)).astype(BF16)
+        second_y[i] = send(half_x.at[i, 1], from_y2.at[i], at_y)
+        first_y[i].wait_recv()
+        half_y[i] = (pair[i, 0, :, :, half:].astype(F32) + from_y[i].astype(F32)).astype(BF16)
+        second_x[i] = send(half_y.at[i, 1], from_x2.at[i], at_x)
+
+    def reduce_third(i):
+        second_y[i].wait_recv()
+        second_x[i].wait_recv()
+        left = half_x[i, 0].astype(F32) + from_y2[i].astype(F32)
+        right = half_y[i, 0].astype(F32) + from_x2[i].astype(F32)
+        plane[i, :, :half] = left.astype(BF16)
+        plane[i, :, half:] = right.astype(BF16)
+        if i:
+            home[i] = send(plane.at[i], from_z.at[i - 1], at_z[i])
+
+    spread(0)
+    for i in (1, 2, 3):
+        along_z[i] = send(rows.at[0, 0, 0], rows.at[i, 0, 0], at_z[i])
+    for i in (1, 2, 3):
+        along_z[i].wait_recv()
+        spread(i)
+        relay(i - 1)
+        if i > 1:
+            close(i - 2)
+    for load in loads:
+        load.wait()
+    arrived(0)
+    relay(3)
+    close(2)
+    arrived(1)
+    expand(0)
+    close(3)
+    hidden(0)
+    back(0)
+    reduce_sibling(0)
+    reduce_sibling(1)
+    arrived(2)
+    arrived(3)
+    expand(2)
+    reduce_first(1)
+    reduce_first(0)
+    hidden(2)
+    reduce_second(1)
+    reduce_second(0)
+    back(2)
+    reduce_sibling(2)
+    reduce_sibling(3)
+    reduce_third(1)
+    reduce_third(0)
+    for i in (2, 3):
+        reduce_first(i)
+    for i in (2, 3):
+        reduce_second(i)
+    for i in (2, 3):
+        reduce_third(i)
+
+    total = plane[0].astype(F32)
+    for i in (1, 2, 3):
+        home[i].wait_recv()
+        total += from_z[i - 1].astype(F32)
+    out_ref[...] = total.astype(BF16)
+    for copy in copies:
+        copy.wait_send()
+
+
+def dense(tokens, cotangent, gates, routes, w_gate, w_up, w_down):
+    tok_dev, width = tokens.shape
+    units = w_gate.shape[1]
+    blocks = lax.axis_size("hid") // EXP_DEV
+    count = 2 * CORES * 4 * tok_dev
+    half = width // 2
+    vmem, anywhere = pl.BlockSpec(memory_space=pltpu.VMEM), pl.BlockSpec(memory_space=pl.ANY)
+    copies = 58
+    return pl.pallas_call(
+        functools.partial(dense_kernel, blocks),
+        out_shape=jax.ShapeDtypeStruct((tok_dev, width), BF16),
+        in_specs=[vmem] * 4 + [anywhere] * 3,
+        out_specs=vmem,
+        scratch_shapes=[
+            pltpu.VMEM((4, CORES, 4, 2 * tok_dev, width + LANES), BF16),
+            pltpu.VMEM((units, width), BF16),
+            pltpu.VMEM((units, width), BF16),
+            pltpu.VMEM((units, width), BF16),
+            pltpu.VMEM((count, width), BF16),
+            pltpu.VMEM((count, units), BF16),
+            pltpu.VMEM((count, units), BF16),
+            pltpu.VMEM((4, CORES, 4, tok_dev, width), BF16),
+            pltpu.VMEM((4, 4, tok_dev, width), BF16),
+            pltpu.VMEM((4, 2, 2, tok_dev, width), BF16),
+            pltpu.VMEM((4, 2, tok_dev, half), BF16),
+            pltpu.VMEM((4, 2, tok_dev, half), BF16),
+            pltpu.VMEM((4, 2, tok_dev, half), BF16),
+            pltpu.VMEM((4, 2, tok_dev, half), BF16),
+            pltpu.VMEM((4, tok_dev, half), BF16),
+            pltpu.VMEM((4, tok_dev, half), BF16),
+            pltpu.VMEM((4, tok_dev, width), BF16),
+            pltpu.VMEM((3, tok_dev, width), BF16),
+            pltpu.SemaphoreType.DMA((3,)),
+            pltpu.SemaphoreType.DMA((copies,)),
+            pltpu.SemaphoreType.DMA((copies,)),
+        ],
+        compiler_params=pltpu.CompilerParams(
+            collective_id=0, has_side_effects=True, vmem_limit_bytes=50 * 1024 * 1024
+        ),
+    )(tokens, cotangent, gates, routes, w_gate, w_up, w_down)
 
 
 def hidden_grad(inputs, cotan, wgate, wup, wdown):
@@ -79,6 +329,7 @@
         P(("ex", "hid"), None, None),
     )
     out_specs = P(("ex", "hid"), None)
+    small = mesh.shape["ex"] == 4 * CORES and mesh.shape["hid"] == 4
     return jax.shard_map(
-        per_device, mesh=mesh, in_specs=in_specs, out_specs=out_specs, check_vma=False
+        dense if small else per_device, mesh=mesh, in_specs=in_specs, out_specs=out_specs, check_vma=False
     )

time: 156 us -> 62.2 us (0.40)
  blocking collectives: 90.8 us -> 0 us
  Pallas kernels: 0 us -> 56.3 us
  local copies, waits for them, and re-layouts: 28.6 us -> 5.64 us
  matrix products: 14 us -> 0 us
  waiting for transfers between devices: 13.6 us -> 0 us
  starting transfers between devices: 4.23 us -> 0 us
  other arithmetic: 3.65 us -> 0 us
    all_to_all x3 -> x0, blocking collectives: 90.8 us -> none  [the longest x1 32.7 us: per_device(): lax.all_to_all(buffer, 'ex', split_axis=2, concat_axis=2, tiled=True)]
    pallas_call x0 -> x1, Pallas kernels: none -> 56.3 us  [dense(): pl.pallas_call(functools.partial(dense_kernel, blocks), out_shape=jax.Sha...]
    dot_general x4 -> x0, matrix products: 14 us -> none  [the longest x1 7.25 us: hidden_grad(): first = jnp.dot(d_gate, wgate, preferred_element_type=jnp.float32)]
    all_to_all x1 -> x0, waiting for transfers between devices: 13.6 us -> none  [per_device(): lax.all_to_all(moved, 'hid', split_axis=0, concat_axis=0, tiled=True)]
    scatter x2 -> x0, local copies, waits for them, and re-layouts: 11.6 us -> none  [per_device(): buffer = jnp.zeros((EXP_DEV, 2, n_ex, slot_cap, width), jnp.bfloat16).at[...]
    broadcast_in_dim x4 -> x0, local copies, waits for them, and re-layouts: 5.44 us -> none  [the longest x1 1.8 us: per_device(): jnp.zeros((EXP_DEV, 2, n_ex, slot_cap, width), jnp.bfloat16)]
    all_to_all x1 -> x0, starting transfers between devices: 4.23 us -> none  [per_device(): lax.all_to_all(moved, 'hid', split_axis=0, concat_axis=0, tiled=True)]
    reduce_sum x3 -> x0, other arithmetic: 2.51 us -> none  [the longest x1 1.39 us: per_device(): jnp.sum(landed.astype(jnp.float32).reshape(EXP_DEV, blocks, n_ex, slot_ca...]
  transfers between devices with their start and end apart: 1 -> 0, of which waited for: 1 -> 0; matrix products, arithmetic and copies ran while one was open for 0% -> 0% of each run, Pallas kernels for 0% -> 0%
where the time goes in v1:
time: 62.2 us; the launch traced here: 61.9 us
  Pallas kernels  56.3 us (91%)
  local copies, waits for them, and re-layouts  5.64 us (9%)
    pallas_call x1, Pallas kernels, dense(): pl.pallas_call(functools.partial(dense_kernel, blocks), out_shape=jax.Sha...  56.3 us
    unnamed x9, local copies, waits for them, and re-layouts  5.64 us

profile of v1, /device:TPU:0, one launch (start us, length us, event | category | flops | bytes accessed | tf_op | source)
XLA Modules:
  0.0 61.9 jit_solution(11267885867978924745)
XLA Ops:
  0.0 0.8 %copy.8.gates_ref = f32[16,4]{1,0:T(8,128)S(1)} copy(f32[16,4]{0,1:T(4,128)} %param.9) | data formatting | bytes 512 | tf_op args[2]
  0.8 0.8 %copy.9.routes_ref = s32[16,4]{1,0:T(8,128)S(1)} copy(s32[16,4]{0,1:T(4,128)} %param.10) | data formatting | bytes 512 | tf_op args[3]
  1.5 0.0 copy-start
  1.5 1.8 %copy-done = bf16[1,704,2048]{2,1,0:T(8,128)(2,1)S(1)} copy-done((bf16[1,704,2048]{2,1,0:T(8,128)(2,1)S(1)}, bf16[1,704,2048]{2,1,0:T(8,128)(2,1)}, u32[]{:S(2)}) %copy-start) | copy-done | bytes 2883608
  3.3 0.0 copy-start.1
  3.3 0.8 %copy-done.1 = bf16[16,2048]{1,0:T(8,128)(2,1)S(1)} copy-done((bf16[16,2048]{1,0:T(8,128)(2,1)S(1)}, bf16[16,2048]{1,0:T(8,128)(2,1)}, u32[]{:S(2)}) %copy-start.1) | copy-done | bytes 65560
  4.2 0.0 copy-start.2
  4.2 0.8 %copy-done.2 = bf16[16,2048]{1,0:T(8,128)(2,1)S(1)} copy-done((bf16[16,2048]{1,0:T(8,128)(2,1)S(1)}, bf16[16,2048]{1,0:T(8,128)(2,1)}, u32[]{:S(2)}) %copy-start.2) | copy-done | bytes 65560
  5.0 56.3 %shard_map.73 = bf16[16,2048]{1,0:T(8,128)(2,1)S(1)} custom-call(bf16[16,2048]{1,0:T(8,128)(2,1)S(1)} %copy-done.1, bf16[16,2048]{1,0:T(8,128)(2,1)S(1)} %copy-done.2, f32[16,4]{1,0:T(8,128)S(1)} %copy.8.gates_ref, s32[16,4]{1,0:T(8,128)S(1)} %copy.9.routes_ref, bf16[1,704,2048]{2,1,0:T(8,128)(2,1)S(1)} %copy-done, bf16[1,704,2048]{2,1,0:T(8,128)(2,1)} %wu_hbm.1, ...), custom_call_target="tpu_custom_call" | custom-call | tf_op jit(solution)/shard_map/pallas_call | solution.py:225
  61.3 0.6 %copy.11 = bf16[16,2048]{1,0:T(8,128)(2,1)} copy(bf16[16,2048]{1,0:T(8,128)(2,1)S(1)} %shard_map.73) | data formatting | bytes 131072
Async XLA Ops:
  1.5 1.8 %copy-start = (bf16[1,704,2048]{2,1,0:T(8,128)(2,1)S(1)}, bf16[1,704,2048]{2,1,0:T(8,128)(2,1)}, u32[]{:S(2)}) copy-start(bf16[1,704,2048]{2,1,0:T(8,128)(2,1)} %wg_hbm.1) | copy-start | bytes 8650756
  3.3 0.8 %copy-start.1 = (bf16[16,2048]{1,0:T(8,128)(2,1)S(1)}, bf16[16,2048]{1,0:T(8,128)(2,1)}, u32[]{:S(2)}) copy-start(bf16[16,2048]{1,0:T(8,128)(2,1)} %tok_ref.1) | copy-start | bytes 196612
  4.2 0.8 %copy-start.2 = (bf16[16,2048]{1,0:T(8,128)(2,1)S(1)}, bf16[16,2048]{1,0:T(8,128)(2,1)}, u32[]{:S(2)}) copy-start(bf16[16,2048]{1,0:T(8,128)(2,1)} %cot_ref.1) | copy-start | bytes 196612

commit v2 on v1

--- a/solution.py
+++ b/solution.py
@@ -16,11 +16,11 @@
 
 def dense_kernel(
     blocks, tok_ref, cot_ref, gates_ref, routes_ref, wg_hbm, wu_hbm, wd_hbm, out_ref,
-    rows, wg, wu, wd, ys, dgs, dus, part, from_sib, pair, from_x, from_y, half_x, half_y,
-    from_y2, from_x2, plane, from_z, w_sem, send_sem, recv_sem,
+    rows, small_g, small_r, wg, wu, wd, xs, ys, gt, ut, dgs, dus, part, from_sib, pair, from_x, from_y,
+    half_x, half_y, from_y2, from_x2, plane, from_z, result, in_sem, w_sem, send_sem, recv_sem,
 ):
     tok_dev, width = tok_ref.shape
-    top = gates_ref.shape[1]
+    top = gates_ref.shape[0]
     half = width // 2
     ex, hid = lax.axis_index("ex"), lax.axis_index("hid")
     z, c = ex // CORES, ex % CORES
@@ -28,6 +28,19 @@
     expert = (ex * lax.axis_size("hid") + hid) // blocks
     experts = EXP_DEV * lax.axis_size("ex")
 
+    first = [
+        pltpu.make_async_copy(src, dst, in_sem.at[i])
+        for i, (src, dst) in enumerate(
+            (
+                (gates_ref, small_g),
+                (routes_ref, small_r),
+                (tok_ref, rows.at[0, 0, 0, pl.ds(0, tok_dev), pl.ds(0, width)]),
+                (cot_ref, rows.at[0, 0, 0, pl.ds(tok_dev, tok_dev), pl.ds(0, width)]),
+            )
+        )
+    ]
+    for load in first:
+        load.start()
     loads = [
         pltpu.make_async_copy(src.at[0], dst, w_sem.at[i])
         for i, (src, dst) in enumerate(((wg_hbm, wg), (wu_hbm, wu), (wd_hbm, wd)))
@@ -50,18 +63,26 @@
 
     lane = lax.broadcasted_iota(jnp.int32, (tok_dev, LANES), 1)
     dense = jnp.zeros((tok_dev, LANES), F32)
+    diagonal = lax.broadcasted_iota(jnp.int32, (tok_dev, tok_dev), 0) == lax.broadcasted_iota(
+        jnp.int32, (tok_dev, tok_dev), 1
+    )
+    place = (lane % experts).astype(F32)
+    first[0].wait()
+    first[1].wait()
     for k in range(top):
-        dense += jnp.where(lane % experts == routes_ref[:, k : k + 1], gates_ref[:, k : k + 1], 0.0)
+        gate_k = jnp.sum(jnp.where(diagonal, small_g[k : k + 1, :], 0.0), axis=1, keepdims=True)
+        route_k = jnp.sum(jnp.where(diagonal, small_r[k : k + 1, :].astype(F32), 0.0), axis=1, keepdims=True)
+        dense += jnp.where(place == route_k, gate_k, 0.0)
     high = dense.astype(BF16).astype(F32)
     rest = dense - high
     mid = rest.astype(BF16).astype(F32)
     low = rest - mid
     term = lane // experts
     terms = jnp.where(term == 0, high, jnp.where(term == 1, mid, jnp.where(term == 2, low, 0.0)))
-    rows[0, 0, 0, :tok_dev, :width] = tok_ref[...]
     rows[0, 0, 0, :tok_dev, width:] = terms.astype(BF16)
-    rows[0, 0, 0, tok_dev:, :width] = cot_ref[...]
     rows[0, 0, 0, tok_dev:, width:] = jnp.zeros((tok_dev, LANES), BF16)
+    first[2].wait()
+    first[3].wait()
     pl.semaphore_wait(barrier, len(partners))
 
     copies = []
@@ -102,49 +123,58 @@
         for r in range(4):
             cross[i, r].wait_recv()
 
+    count = 2 * CORES * 4 * tok_dev
+    units = wg.shape[0]
+    rhs_last = (((1,), (1,)), ((), ()))
+
     def expand(i):
-        count = 2 * CORES * 4 * tok_dev
         gate_rows = rows[pl.ds(i, 2), :, :, pl.ds(0, tok_dev), pl.ds(width, LANES)].reshape(count, LANES)
         lanes = lax.broadcasted_iota(jnp.int32, (count, LANES), 1)
         mine = (lanes % experts == expert) & (lanes < 3 * experts)
         gate = jnp.sum(jnp.where(mine, gate_rows.astype(F32), 0.0), axis=1, keepdims=True)
         cot = rows[pl.ds(i, 2), :, :, pl.ds(tok_dev, tok_dev), pl.ds(0, width)].reshape(count, width)
         ys[...] = (gate * cot.astype(F32)).astype(BF16)
-
-    def hidden(i):
-        count = 2 * CORES * 4 * tok_dev
-        dims = (((1,), (1,)), ((), ()))
-        inputs = rows[pl.ds(i, 2), :, :, pl.ds(0, tok_dev), pl.ds(0, width)].reshape(count, width)
-        gate = lax.dot_general(inputs, wg[...], dims, preferred_element_type=F32)
-        upper = lax.dot_general(inputs, wu[...], dims, preferred_element_type=F32)
-        down = lax.dot_general(ys[...], wd[...], dims, preferred_element_type=F32)
+        xs[...] = rows[pl.ds(i, 2), :, :, pl.ds(0, tok_dev), pl.ds(0, width)].reshape(count, width)
+
+    def product_gate():
+        gt[...] = lax.dot_general(wg[...], xs[...], rhs_last, preferred_element_type=F32)
+
+    def product_up():
+        ut[...] = lax.dot_general(wu[...], xs[...], rhs_last, preferred_element_type=F32)
+
+    def product_down():
+        down = lax.dot_general(wd[...], ys[...], rhs_last, preferred_element_type=F32)
+        gate = gt[...]
         sig = jax.nn.sigmoid(gate)
-        dus[...] = (down * gate * sig).astype(BF16)
-        dgs[...] = (down * upper * sig * (1.0 + gate * (1.0 - sig))).astype(BF16)
-
-    def back(i):
-        step = width // 4
+        dus[...] = (down * gate * sig).T.astype(BF16)
+        dgs[...] = (down * ut[...] * sig * (1.0 + gate * (1.0 - sig))).T.astype(BF16)
+
+    def back(i, which):
+        step = half // 2
 
         def body(n, carry):
-            at = pl.ds(pl.multiple_of(n * step, step), step)
+            at = pl.ds(pl.multiple_of(which * half + n * step, step), step)
             value = jnp.dot(dgs[...], wg[:, at], preferred_element_type=F32)
             value += jnp.dot(dus[...], wu[:, at], preferred_element_type=F32)
             part[pl.ds(i, 2), :, :, :, at] = value.astype(BF16).reshape(2, CORES, 4, tok_dev, step)
             return carry
 
-        lax.fori_loop(0, 4, body, 0)
+        lax.fori_loop(0, 2, body, 0)
+        for k in (i + 1, i):
+            at = pl.ds(which * half, half)
+            sib[k, which] = send(part.at[k, 1, :, :, at], from_sib.at[k, :, :, at], sibling)
 
     sib, first_x, first_y, second_x, second_y, home = {}, {}, {}, {}, {}, {}
 
-    def reduce_sibling(i):
-        sib[i] = send(part.at[i, 1], from_sib.at[i], sibling)
-
-    def reduce_first(i):
-        sib[i].wait_recv()
-        total = part[i, 0].astype(F32) + from_sib[i].astype(F32)
-        pair[i] = total.astype(BF16).reshape(2, 2, tok_dev, width)
-        first_x[i] = send(pair.at[i, :, 1, :, pl.ds(0, half)], from_x.at[i], at_x)
-        first_y[i] = send(pair.at[i, 1, :, :, pl.ds(half, half)], from_y.at[i], at_y)
+    def reduce_first(i, which):
+        sib[i, which].wait_recv()
+        at = pl.ds(which * half, half)
+        total = part[i, 0, :, :, at].astype(F32) + from_sib[i, :, :, at].astype(F32)
+        pair[i, :, :, :, at] = total.astype(BF16).reshape(2, 2, tok_dev, half)
+        if which == 0:
+            first_x[i] = send(pair.at[i, :, 1, :, at], from_x.at[i], at_x)
+        else:
+            first_y[i] = send(pair.at[i, 1, :, :, at], from_y.at[i], at_y)
 
     def reduce_second(i):
         first_x[i].wait_recv()
@@ -167,51 +197,60 @@
     spread(0)
     for i in (1, 2, 3):
         along_z[i] = send(rows.at[0, 0, 0], rows.at[i, 0, 0], at_z[i])
-    for i in (1, 2, 3):
+    for i in (1, 2):
         along_z[i].wait_recv()
         spread(i)
         relay(i - 1)
-        if i > 1:
-            close(i - 2)
+    close(0)
+    along_z[3].wait_recv()
+    spread(3)
+    close(1)
+    arrived(0)
+    arrived(1)
+    expand(0)
     for load in loads:
         load.wait()
-    arrived(0)
+    relay(2)
+    product_gate()
+    product_up()
+    close(2)
     relay(3)
-    close(2)
-    arrived(1)
-    expand(0)
+    product_down()
     close(3)
-    hidden(0)
-    back(0)
-    reduce_sibling(0)
-    reduce_sibling(1)
+    back(0, 0)
+    back(0, 1)
+    for i in (1, 0):
+        reduce_first(i, 0)
+        reduce_first(i, 1)
     arrived(2)
     arrived(3)
     expand(2)
-    reduce_first(1)
-    reduce_first(0)
-    hidden(2)
+    product_gate()
     reduce_second(1)
+    product_up()
     reduce_second(0)
-    back(2)
-    reduce_sibling(2)
-    reduce_sibling(3)
+    product_down()
     reduce_third(1)
     reduce_third(0)
-    for i in (2, 3):
-        reduce_first(i)
-    for i in (2, 3):
+    back(2, 0)
+    back(2, 1)
+    for which in (0, 1):
+        reduce_first(3, which)
+        reduce_first(2, which)
+    for i in (3, 2):
         reduce_second(i)
-    for i in (2, 3):
+    for i in (3, 2):
         reduce_third(i)
-
     total = plane[0].astype(F32)
     for i in (1, 2, 3):
         home[i].wait_recv()
         total += from_z[i - 1].astype(F32)
-    out_ref[...] = total.astype(BF16)
+    result[...] = total.astype(BF16)
+    store = pltpu.make_async_copy(result, out_ref, in_sem.at[0])
+    store.start()
     for copy in copies:
         copy.wait_send()
+    store.wait()
 
 
 def dense(tokens, cotangent, gates, routes, w_gate, w_up, w_down):
@@ -220,19 +259,25 @@
     blocks = lax.axis_size("hid") // EXP_DEV
     count = 2 * CORES * 4 * tok_dev
     half = width // 2
-    vmem, anywhere = pl.BlockSpec(memory_space=pltpu.VMEM), pl.BlockSpec(memory_space=pl.ANY)
-    copies = 58
+    top = gates.shape[1]
+    hbm = pl.BlockSpec(memory_space=pltpu.HBM)
+    copies = 62
     return pl.pallas_call(
         functools.partial(dense_kernel, blocks),
         out_shape=jax.ShapeDtypeStruct((tok_dev, width), BF16),
-        in_specs=[vmem] * 4 + [anywhere] * 3,
-        out_specs=vmem,
+        in_specs=[hbm] * 7,
+        out_specs=hbm,
         scratch_shapes=[
             pltpu.VMEM((4, CORES, 4, 2 * tok_dev, width + LANES), BF16),
+            pltpu.VMEM((top, tok_dev), F32),
+            pltpu.VMEM((top, tok_dev), jnp.int32),
             pltpu.VMEM((units, width), BF16),
             pltpu.VMEM((units, width), BF16),
             pltpu.VMEM((units, width), BF16),
             pltpu.VMEM((count, width), BF16),
+            pltpu.VMEM((count, width), BF16),
+            pltpu.VMEM((units, count), F32),
+            pltpu.VMEM((units, count), F32),
             pltpu.VMEM((count, units), BF16),
             pltpu.VMEM((count, units), BF16),
             pltpu.VMEM((4, CORES, 4, tok_dev, width), BF16),
@@ -246,14 +291,16 @@
             pltpu.VMEM((4, tok_dev, half), BF16),
             pltpu.VMEM((4, tok_dev, width), BF16),
             pltpu.VMEM((3, tok_dev, width), BF16),
+            pltpu.VMEM((tok_dev, width), BF16),
+            pltpu.SemaphoreType.DMA((4,)),
             pltpu.SemaphoreType.DMA((3,)),
             pltpu.SemaphoreType.DMA((copies,)),
             pltpu.SemaphoreType.DMA((copies,)),
         ],
         compiler_params=pltpu.CompilerParams(
-            collective_id=0, has_side_effects=True, vmem_limit_bytes=50 * 1024 * 1024
+            collective_id=0, has_side_effects=True, vmem_limit_bytes=60 * 1024 * 1024
         ),
-    )(tokens, cotangent, gates, routes, w_gate, w_up, w_down)
+    )(tokens, cotangent, gates.T, routes.T, w_gate, w_up, w_down)
 
 
 def hidden_grad(inputs, cotan, wgate, wup, wdown):

time: 62.2 us -> 62.3 us (level)
  Pallas kernels: 56.3 us -> 60.6 us
  local copies, waits for them, and re-layouts: 5.64 us -> 1.47 us
    pallas_call x1, Pallas kernels: 56.3 us -> 60.6 us  [dense(): pl.pallas_call(functools.partial(dense_kernel, blocks), out_shape=jax.Sha...]
    unnamed x9 -> x1, local copies, waits for them, and re-layouts: 5.64 us -> 1.47 us
where the time goes in v2:
time: 62.3 us; the launch traced here: 62.1 us
  Pallas kernels  60.6 us (97%)
  local copies, waits for them, and re-layouts  1.47 us (2%)
    pallas_call x1, Pallas kernels, dense(): pl.pallas_call(functools.partial(dense_kernel, blocks), out_shape=jax.Sha...  60.6 us
    unnamed x1, local copies, waits for them, and re-layouts  1.47 us

profile of v2, /device:TPU:0, one launch (start us, length us, event | category | flops | bytes accessed | tf_op | source)
XLA Modules:
  0.0 62.1 jit_solution(8136005621661421885)
XLA Ops:
  0.0 60.6 %shard_map.73 = bf16[16,2048]{1,0:T(8,128)(2,1)} custom-call(bf16[16,2048]{1,0:T(8,128)(2,1)} %tok_ref.1, bf16[16,2048]{1,0:T(8,128)(2,1)} %cot_ref.1, f32[4,16]{1,0:T(4,128)} %bitcast.2, s32[4,16]{1,0:T(4,128)} %bitcast.3, bf16[1,704,2048]{2,1,0:T(8,128)(2,1)} %wg_hbm.1, bf16[1,704,2048]{2,1,0:T(8,128)(2,1)} %wu_hbm.1, bf16[1,704,2048]{2,1,0:T(8,128)(2,1)} %wd_hbm.1), custom_call_target="tpu_custom_call" | custom-call | tf_op jit(solution)/shard_map/pallas_call | solution.py:265
  60.6 1.5 %copy.9 = bf16[16,2048]{1,0:T(8,128)(2,1)} copy(bf16[16,2048]{1,0:T(8,128)(2,1)} %shard_map.73) | data formatting | bytes 131072

commit v3 on v2

--- a/solution.py
+++ b/solution.py
@@ -10,17 +10,19 @@
 EXP_DEV = 2
 CORES = 2
 LANES = 128
+TILE = 256
 F32 = jnp.float32
 BF16 = jnp.bfloat16
 
 
 def dense_kernel(
     blocks, tok_ref, cot_ref, gates_ref, routes_ref, wg_hbm, wu_hbm, wd_hbm, out_ref,
-    rows, small_g, small_r, wg, wu, wd, xs, ys, gt, ut, dgs, dus, part, from_sib, pair, from_x, from_y,
-    half_x, half_y, from_y2, from_x2, plane, from_z, result, in_sem, w_sem, send_sem, recv_sem,
+    rows, small_g, small_r, wg, wu, wd, xs, ys, dgs, dus, part, from_sib, pair, from_x, from_y,
+    half_x, half_y, from_y2, from_x2, plane, from_z, in_sem, w_sem, send_sem, recv_sem,
 ):
     tok_dev, width = tok_ref.shape
     top = gates_ref.shape[0]
+    units = wg_hbm.shape[1]
     half = width // 2
     ex, hid = lax.axis_index("ex"), lax.axis_index("hid")
     z, c = ex // CORES, ex % CORES
@@ -34,19 +36,22 @@
             (
                 (gates_ref, small_g),
                 (routes_ref, small_r),
-                (tok_ref, rows.at[0, 0, 0, pl.ds(0, tok_dev), pl.ds(0, width)]),
-                (cot_ref, rows.at[0, 0, 0, pl.ds(tok_dev, tok_dev), pl.ds(0, width)]),
+                (tok_ref, rows.at[0, 0, 0, :, pl.ds(0, width)]),
+                (cot_ref, rows.at[0, 0, 0, :, pl.ds(width, width)]),
             )
         )
     ]
     for load in first:
         load.start()
     loads = [
-        pltpu.make_async_copy(src.at[0], dst, w_sem.at[i])
+        pltpu.make_async_copy(src.at[0], dst.at[pl.ds(0, units)], w_sem.at[i])
         for i, (src, dst) in enumerate(((wg_hbm, wg), (wu_hbm, wu), (wd_hbm, wd)))
     ]
     for load in loads:
         load.start()
+    padded = wg.shape[0]
+    for weight in (wg, wu, wd):
+        weight[units:] = jnp.zeros((padded - units, width), BF16)
 
     def device(zz, cc, yy, xx):
         return (zz * CORES + cc, yy * 2 + xx)
@@ -79,8 +84,7 @@
     low = rest - mid
     term = lane // experts
     terms = jnp.where(term == 0, high, jnp.where(term == 1, mid, jnp.where(term == 2, low, 0.0)))
-    rows[0, 0, 0, :tok_dev, width:] = terms.astype(BF16)
-    rows[0, 0, 0, tok_dev:, width:] = jnp.zeros((tok_dev, LANES), BF16)
+    rows[0, 0, 0, :, 2 * width :] = terms.astype(BF16)
     first[2].wait()
     first[3].wait()
     pl.semaphore_wait(barrier, len(partners))
@@ -106,11 +110,11 @@
 
     def relay(i):
         along_x[i].wait_recv()
-        diag_y[i] = send(rows.at[i, 0, 1, pl.ds(0, tok_dev)], rows.at[i, 0, 3, pl.ds(0, tok_dev)], at_y)
+        diag_y[i] = send(rows.at[i, 0, 1, :, pl.ds(0, width)], rows.at[i, 0, 3, :, pl.ds(0, width)], at_y)
         cross[i, 1] = send(rows.at[i, 0, 1], rows.at[i, 1, 1], sibling)
         along_y[i].wait_recv()
         diag_x[i] = send(
-            rows.at[i, 0, 2, pl.ds(tok_dev, tok_dev)], rows.at[i, 0, 3, pl.ds(tok_dev, tok_dev)], at_x
+            rows.at[i, 0, 2, :, pl.ds(width, width + LANES)], rows.at[i, 0, 3, :, pl.ds(width, width + LANES)], at_x
         )
         cross[i, 2] = send(rows.at[i, 0, 2], rows.at[i, 1, 2], sibling)
 
@@ -124,30 +128,29 @@
             cross[i, r].wait_recv()
 
     count = 2 * CORES * 4 * tok_dev
-    units = wg.shape[0]
     rhs_last = (((1,), (1,)), ((), ()))
 
     def expand(i):
-        gate_rows = rows[pl.ds(i, 2), :, :, pl.ds(0, tok_dev), pl.ds(width, LANES)].reshape(count, LANES)
+        gate_rows = rows[pl.ds(i, 2), :, :, :, pl.ds(2 * width, LANES)].reshape(count, LANES)
         lanes = lax.broadcasted_iota(jnp.int32, (count, LANES), 1)
         mine = (lanes % experts == expert) & (lanes < 3 * experts)
         gate = jnp.sum(jnp.where(mine, gate_rows.astype(F32), 0.0), axis=1, keepdims=True)
-        cot = rows[pl.ds(i, 2), :, :, pl.ds(tok_dev, tok_dev), pl.ds(0, width)].reshape(count, width)
+        cot = rows[pl.ds(i, 2), :, :, :, pl.ds(width, width)].reshape(count, width)
         ys[...] = (gate * cot.astype(F32)).astype(BF16)
-        xs[...] = rows[pl.ds(i, 2), :, :, pl.ds(0, tok_dev), pl.ds(0, width)].reshape(count, width)
-
-    def product_gate():
-        gt[...] = lax.dot_general(wg[...], xs[...], rhs_last, preferred_element_type=F32)
-
-    def product_up():
-        ut[...] = lax.dot_general(wu[...], xs[...], rhs_last, preferred_element_type=F32)
-
-    def product_down():
-        down = lax.dot_general(wd[...], ys[...], rhs_last, preferred_element_type=F32)
-        gate = gt[...]
-        sig = jax.nn.sigmoid(gate)
-        dus[...] = (down * gate * sig).T.astype(BF16)
-        dgs[...] = (down * ut[...] * sig * (1.0 + gate * (1.0 - sig))).T.astype(BF16)
+        xs[...] = rows[pl.ds(i, 2), :, :, :, pl.ds(0, width)].reshape(count, width)
+
+    def forward():
+        def body(n, carry):
+            at = pl.ds(pl.multiple_of(n * TILE, TILE), TILE)
+            gate = lax.dot_general(xs[...], wg[at, :], rhs_last, preferred_element_type=F32)
+            upper = lax.dot_general(xs[...], wu[at, :], rhs_last, preferred_element_type=F32)
+            down = lax.dot_general(ys[...], wd[at, :], rhs_last, preferred_element_type=F32)
+            sig = jax.nn.sigmoid(gate)
+            dus[:, at] = (down * gate * sig).astype(BF16)
+            dgs[:, at] = (down * upper * sig * (1.0 + gate * (1.0 - sig))).astype(BF16)
+            return carry
+
+        lax.fori_loop(0, padded // TILE, body, 0)
 
     def back(i, which):
         step = half // 2
@@ -205,34 +208,30 @@
     along_z[3].wait_recv()
     spread(3)
     close(1)
+    relay(2)
     arrived(0)
     arrived(1)
     expand(0)
     for load in loads:
         load.wait()
-    relay(2)
-    product_gate()
-    product_up()
+    forward()
+    relay(3)
     close(2)
-    relay(3)
-    product_down()
-    close(3)
     back(0, 0)
     back(0, 1)
+    close(3)
     for i in (1, 0):
         reduce_first(i, 0)
         reduce_first(i, 1)
     arrived(2)
     arrived(3)
     expand(2)
-    product_gate()
+    forward()
     reduce_second(1)
-    product_up()
     reduce_second(0)
-    product_down()
+    back(2, 0)
     reduce_third(1)
     reduce_third(0)
-    back(2, 0)
     back(2, 1)
     for which in (0, 1):
         reduce_first(3, which)
@@ -245,17 +244,14 @@
     for i in (1, 2, 3):
         home[i].wait_recv()
         total += from_z[i - 1].astype(F32)
-    result[...] = total.astype(BF16)
-    store = pltpu.make_async_copy(result, out_ref, in_sem.at[0])
-    store.start()
+    out_ref[...] = total.astype(BF16)
     for copy in copies:
         copy.wait_send()
-    store.wait()
 
 
 def dense(tokens, cotangent, gates, routes, w_gate, w_up, w_down):
     tok_dev, width = tokens.shape
-    units = w_gate.shape[1]
+    padded = -(-w_gate.shape[1] // TILE) * TILE
     blocks = lax.axis_size("hid") // EXP_DEV
     count = 2 * CORES * 4 * tok_dev
     half = width // 2
@@ -266,20 +262,18 @@
         functools.partial(dense_kernel, blocks),
         out_shape=jax.ShapeDtypeStruct((tok_dev, width), BF16),
         in_specs=[hbm] * 7,
-        out_specs=hbm,
+        out_specs=pl.BlockSpec(memory_space=pltpu.VMEM),
         scratch_shapes=[
-            pltpu.VMEM((4, CORES, 4, 2 * tok_dev, width + LANES), BF16),
+            pltpu.VMEM((4, CORES, 4, tok_dev, 2 * width + LANES), BF16),
             pltpu.VMEM((top, tok_dev), F32),
             pltpu.VMEM((top, tok_dev), jnp.int32),
-            pltpu.VMEM((units, width), BF16),
-            pltpu.VMEM((units, width), BF16),
-            pltpu.VMEM((units, width), BF16),
+            pltpu.VMEM((padded, width), BF16),
+            pltpu.VMEM((padded, width), BF16),
+            pltpu.VMEM((padded, width), BF16),
             pltpu.VMEM((count, width), BF16),
             pltpu.VMEM((count, width), BF16),
-            pltpu.VMEM((units, count), F32),
-            pltpu.VMEM((units, count), F32),
-            pltpu.VMEM((count, units), BF16),
-            pltpu.VMEM((count, units), BF16),
+            pltpu.VMEM((count, padded), BF16),
+            pltpu.VMEM((count, padded), BF16),
             pltpu.VMEM((4, CORES, 4, tok_dev, width), BF16),
             pltpu.VMEM((4, 4, tok_dev, width), BF16),
             pltpu.VMEM((4, 2, 2, tok_dev, width), BF16),
@@ -291,7 +285,6 @@
             pltpu.VMEM((4, tok_dev, half), BF16),
             pltpu.VMEM((4, tok_dev, width), BF16),
             pltpu.VMEM((3, tok_dev, width), BF16),
-            pltpu.VMEM((tok_dev, width), BF16),
             pltpu.SemaphoreType.DMA((4,)),
             pltpu.SemaphoreType.DMA((3,)),
             pltpu.SemaphoreType.DMA((copies,)),

time: 62.3 us -> 57.2 us (0.918)
  Pallas kernels: 60.6 us -> 55.5 us
    pallas_call x1, Pallas kernels: 60.6 us -> 55.5 us  [dense(): pl.pallas_call(functools.partial(dense_kernel, blocks), out_shape=jax.Sha...]
where the time goes in v3:
time: 57.2 us; the launch traced here: 57 us
  Pallas kernels  55.5 us (97%)
  local copies, waits for them, and re-layouts  1.47 us (3%)
    pallas_call x1, Pallas kernels, dense(): pl.pallas_call(functools.partial(dense_kernel, blocks), out_shape=jax.Sha...  55.5 us
    unnamed x1, local copies, waits for them, and re-layouts  1.47 us

profile of v3, /device:TPU:0, one launch (start us, length us, event | category | flops | bytes accessed | tf_op | source)
XLA Modules:
  0.0 57.0 jit_solution(5946536257054768980)
XLA Ops:
  0.0 55.5 %shard_map.73 = bf16[16,2048]{1,0:T(8,128)(2,1)} custom-call(bf16[16,2048]{1,0:T(8,128)(2,1)} %tok_ref.1, bf16[16,2048]{1,0:T(8,128)(2,1)} %cot_ref.1, f32[4,16]{1,0:T(4,128)} %bitcast.2, s32[4,16]{1,0:T(4,128)} %bitcast.3, bf16[1,704,2048]{2,1,0:T(8,128)(2,1)} %wg_hbm.1, bf16[1,704,2048]{2,1,0:T(8,128)(2,1)} %wu_hbm.1, bf16[1,704,2048]{2,1,0:T(8,128)(2,1)} %wd_hbm.1), custom_call_target="tpu_custom_call" | custom-call | tf_op jit(solution)/shard_map/pallas_call | solution.py:261
  55.5 1.5 %copy.9 = bf16[16,2048]{1,0:T(8,128)(2,1)} copy(bf16[16,2048]{1,0:T(8,128)(2,1)} %shard_map.73) | data formatting | bytes 131072

commit v4 on v3

--- a/solution.py
+++ b/solution.py
@@ -29,6 +29,19 @@
     y, x = hid // 2, hid % 2
     expert = (ex * lax.axis_size("hid") + hid) // blocks
     experts = EXP_DEV * lax.axis_size("ex")
+
+    def device(zz, cc, yy, xx):
+        return (zz * CORES + cc, yy * 2 + xx)
+
+    z_of = (z, z + 1 - 2 * (z % 2), (z + 2) % 4, 3 - z)
+    at_x = device(z, c, y, 1 - x)
+    at_y = device(z, c, 1 - y, x)
+    sibling = device(z, 1 - c, y, x)
+    at_z = [device(zz, c, y, x) for zz in z_of]
+    partners = [at_x, at_y, sibling] + at_z[1:]
+    barrier = pltpu.get_barrier_semaphore()
+    for partner in partners:
+        pl.semaphore_signal(barrier, inc=1, device_id=partner, device_id_type=pl.DeviceIdType.MESH)
 
     first = [
         pltpu.make_async_copy(src, dst, in_sem.at[i])
@@ -53,19 +66,6 @@
     for weight in (wg, wu, wd):
         weight[units:] = jnp.zeros((padded - units, width), BF16)
 
-    def device(zz, cc, yy, xx):
-        return (zz * CORES + cc, yy * 2 + xx)
-
-    z_of = (z, z + 1 - 2 * (z % 2), (z + 2) % 4, 3 - z)
-    at_x = device(z, c, y, 1 - x)
-    at_y = device(z, c, 1 - y, x)
-    sibling = device(z, 1 - c, y, x)
-    at_z = [device(zz, c, y, x) for zz in z_of]
-    partners = [at_x, at_y, sibling] + at_z[1:]
-    barrier = pltpu.get_barrier_semaphore()
-    for partner in partners:
-        pl.semaphore_signal(barrier, inc=1, device_id=partner, device_id_type=pl.DeviceIdType.MESH)
-
     lane = lax.broadcasted_iota(jnp.int32, (tok_dev, LANES), 1)
     dense = jnp.zeros((tok_dev, LANES), F32)
     diagonal = lax.broadcasted_iota(jnp.int32, (tok_dev, tok_dev), 0) == lax.broadcasted_iota(
@@ -101,7 +101,7 @@
         copies.append(copy)
         return copy
 
-    along_z, along_x, along_y, diag_x, diag_y, cross = [None] * 4, [None] * 4, [None] * 4, [None] * 4, [None] * 4, {}
+    along_z, along_x, along_y, diag_x, diag_y, diag_z, cross = {}, {}, {}, {}, {}, {}, {}
 
     def spread(i):
         along_x[i] = send(rows.at[i, 0, 0], rows.at[i, 0, 1], at_x)
@@ -110,17 +110,22 @@
 
     def relay(i):
         along_x[i].wait_recv()
-        diag_y[i] = send(rows.at[i, 0, 1, :, pl.ds(0, width)], rows.at[i, 0, 3, :, pl.ds(0, width)], at_y)
+        if i % 2 == 0:
+            diag_y[i] = send(rows.at[i, 0, 1, :, pl.ds(0, width)], rows.at[i, 0, 3, :, pl.ds(0, width)], at_y)
         cross[i, 1] = send(rows.at[i, 0, 1], rows.at[i, 1, 1], sibling)
         along_y[i].wait_recv()
-        diag_x[i] = send(
-            rows.at[i, 0, 2, :, pl.ds(width, width + LANES)], rows.at[i, 0, 3, :, pl.ds(width, width + LANES)], at_x
-        )
+        if i % 2 == 0:
+            rest_of = pl.ds(width, width + LANES)
+            diag_x[i] = send(rows.at[i, 0, 2, :, rest_of], rows.at[i, 0, 3, :, rest_of], at_x)
         cross[i, 2] = send(rows.at[i, 0, 2], rows.at[i, 1, 2], sibling)
 
     def close(i):
-        diag_y[i].wait_recv()
-        diag_x[i].wait_recv()
+        if i % 2 == 0:
+            diag_y[i].wait_recv()
+            diag_x[i].wait_recv()
+            diag_z[i + 1] = send(rows.at[i, 0, 3], rows.at[i + 1, 0, 3], at_z[1])
+        else:
+            diag_z[i].wait_recv()
         cross[i, 3] = send(rows.at[i, 0, 3], rows.at[i, 1, 3], sibling)
 
     def arrived(i):
@@ -139,7 +144,7 @@
         ys[...] = (gate * cot.astype(F32)).astype(BF16)
         xs[...] = rows[pl.ds(i, 2), :, :, :, pl.ds(0, width)].reshape(count, width)
 
-    def forward():
+    def forward(low, high):
         def body(n, carry):
             at = pl.ds(pl.multiple_of(n * TILE, TILE), TILE)
             gate = lax.dot_general(xs[...], wg[at, :], rhs_last, preferred_element_type=F32)
@@ -150,7 +155,7 @@
             dgs[:, at] = (down * upper * sig * (1.0 + gate * (1.0 - sig))).astype(BF16)
             return carry
 
-        lax.fori_loop(0, padded // TILE, body, 0)
+        lax.fori_loop(low, high, body, 0)
 
     def back(i, which):
         step = half // 2
@@ -192,41 +197,49 @@
         second_x[i].wait_recv()
         left = half_x[i, 0].astype(F32) + from_y2[i].astype(F32)
         right = half_y[i, 0].astype(F32) + from_x2[i].astype(F32)
+        if i == 2:
+            home[3].wait_recv()
+            left += from_z[2, :, :half].astype(F32)
+            right += from_z[2, :, half:].astype(F32)
         plane[i, :, :half] = left.astype(BF16)
         plane[i, :, half:] = right.astype(BF16)
         if i:
-            home[i] = send(plane.at[i], from_z.at[i - 1], at_z[i])
-
+            home[i] = send(plane.at[i], from_z.at[i - 1], at_z[2 if i == 2 else 1])
+
+    tiles = padded // TILE
     spread(0)
     for i in (1, 2, 3):
         along_z[i] = send(rows.at[0, 0, 0], rows.at[i, 0, 0], at_z[i])
-    for i in (1, 2):
-        along_z[i].wait_recv()
-        spread(i)
-        relay(i - 1)
+    along_z[1].wait_recv()
+    spread(1)
+    relay(0)
+    relay(1)
     close(0)
+    along_z[2].wait_recv()
+    spread(2)
+    close(1)
+    relay(2)
     along_z[3].wait_recv()
     spread(3)
-    close(1)
-    relay(2)
     arrived(0)
     arrived(1)
     expand(0)
     for load in loads:
         load.wait()
-    forward()
+    forward(0, 1)
+    close(2)
+    forward(1, tiles)
     relay(3)
-    close(2)
     back(0, 0)
+    close(3)
     back(0, 1)
-    close(3)
     for i in (1, 0):
         reduce_first(i, 0)
         reduce_first(i, 1)
     arrived(2)
     arrived(3)
     expand(2)
-    forward()
+    forward(0, tiles)
     reduce_second(1)
     reduce_second(0)
     back(2, 0)
@@ -241,7 +254,7 @@
     for i in (3, 2):
         reduce_third(i)
     total = plane[0].astype(F32)
-    for i in (1, 2, 3):
+    for i in (1, 2):
         home[i].wait_recv()
         total += from_z[i - 1].astype(F32)
     out_ref[...] = total.astype(BF16)
@@ -257,7 +270,7 @@
     half = width // 2
     top = gates.shape[1]
     hbm = pl.BlockSpec(memory_space=pltpu.HBM)
-    copies = 62
+    copies = 60
     return pl.pallas_call(
         functools.partial(dense_kernel, blocks),
         out_shape=jax.ShapeDtypeStruct((tok_dev, width), BF16),

time: 57.2 us -> 61 us (1.066)
  Pallas kernels: 55.5 us -> 59.3 us
    pallas_call x1, Pallas kernels: 55.5 us -> 59.3 us  [dense(): pl.pallas_call(functools.partial(dense_kernel, blocks), out_shape=jax.Sha...]
where the time goes in v4:
time: 61 us; the launch traced here: 60.8 us
  Pallas kernels  59.3 us (97%)
  local copies, waits for them, and re-layouts  1.47 us (2%)
    pallas_call x1, Pallas kernels, dense(): pl.pallas_call(functools.partial(dense_kernel, blocks), out_shape=jax.Sha...  59.3 us
    unnamed x1, local copies, waits for them, and re-layouts  1.47 us

profile of v4, /device:TPU:0, one launch (start us, length us, event | category | flops | bytes accessed | tf_op | source)
XLA Modules:
  0.0 60.8 jit_solution(2789540052080133730)
XLA Ops:
  0.0 59.3 %shard_map.73 = bf16[16,2048]{1,0:T(8,128)(2,1)} custom-call(bf16[16,2048]{1,0:T(8,128)(2,1)} %tok_ref.1, bf16[16,2048]{1,0:T(8,128)(2,1)} %cot_ref.1, f32[4,16]{1,0:T(4,128)} %bitcast.2, s32[4,16]{1,0:T(4,128)} %bitcast.3, bf16[1,704,2048]{2,1,0:T(8,128)(2,1)} %wg_hbm.1, bf16[1,704,2048]{2,1,0:T(8,128)(2,1)} %wu_hbm.1, bf16[1,704,2048]{2,1,0:T(8,128)(2,1)} %wd_hbm.1), custom_call_target="tpu_custom_call" | custom-call | tf_op jit(solution)/shard_map/pallas_call | solution.py:274
  59.3 1.5 %copy.9 = bf16[16,2048]{1,0:T(8,128)(2,1)} copy(bf16[16,2048]{1,0:T(8,128)(2,1)} %shard_map.73) | data formatting | bytes 131072

commit v5 on v3

--- a/solution.py
+++ b/solution.py
@@ -17,7 +17,7 @@
 
 def dense_kernel(
     blocks, tok_ref, cot_ref, gates_ref, routes_ref, wg_hbm, wu_hbm, wd_hbm, out_ref,
-    rows, small_g, small_r, wg, wu, wd, xs, ys, dgs, dus, part, from_sib, pair, from_x, from_y,
+    rows, small_g, small_r, wg, wu, wd, wgt, wut, wdt, xs, ys, dgs, dus, part, from_sib, pair, from_x, from_y,
     half_x, half_y, from_y2, from_x2, plane, from_z, in_sem, w_sem, send_sem, recv_sem,
 ):
     tok_dev, width = tok_ref.shape
@@ -128,7 +128,6 @@
             cross[i, r].wait_recv()
 
     count = 2 * CORES * 4 * tok_dev
-    rhs_last = (((1,), (1,)), ((), ()))
 
     def expand(i):
         gate_rows = rows[pl.ds(i, 2), :, :, :, pl.ds(2 * width, LANES)].reshape(count, LANES)
@@ -139,12 +138,23 @@
         ys[...] = (gate * cot.astype(F32)).astype(BF16)
         xs[...] = rows[pl.ds(i, 2), :, :, :, pl.ds(0, width)].reshape(count, width)
 
+    def turn(k):
+        loads[k].wait()
+        src, dst = ((wg, wgt), (wu, wut), (wd, wdt))[k]
+
+        def body(n, carry):
+            at = pl.ds(pl.multiple_of(n * TILE, TILE), TILE)
+            dst[:, at] = src[at, :].T
+            return carry
+
+        lax.fori_loop(0, padded // TILE, body, 0)
+
     def forward():
         def body(n, carry):
             at = pl.ds(pl.multiple_of(n * TILE, TILE), TILE)
-            gate = lax.dot_general(xs[...], wg[at, :], rhs_last, preferred_element_type=F32)
-            upper = lax.dot_general(xs[...], wu[at, :], rhs_last, preferred_element_type=F32)
-            down = lax.dot_general(ys[...], wd[at, :], rhs_last, preferred_element_type=F32)
+            gate = jnp.dot(xs[...], wgt[:, at], preferred_element_type=F32)
+            upper = jnp.dot(xs[...], wut[:, at], preferred_element_type=F32)
+            down = jnp.dot(ys[...], wdt[:, at], preferred_element_type=F32)
             sig = jax.nn.sigmoid(gate)
             dus[:, at] = (down * gate * sig).astype(BF16)
             dgs[:, at] = (down * upper * sig * (1.0 + gate * (1.0 - sig))).astype(BF16)
@@ -200,10 +210,12 @@
     spread(0)
     for i in (1, 2, 3):
         along_z[i] = send(rows.at[0, 0, 0], rows.at[i, 0, 0], at_z[i])
+    turn(0)
     for i in (1, 2):
         along_z[i].wait_recv()
         spread(i)
         relay(i - 1)
+        turn(i)
     close(0)
     along_z[3].wait_recv()
     spread(3)
@@ -212,8 +224,6 @@
     arrived(0)
     arrived(1)
     expand(0)
-    for load in loads:
-        load.wait()
     forward()
     relay(3)
     close(2)
@@ -270,6 +280,9 @@
             pltpu.VMEM((padded, width), BF16),
             pltpu.VMEM((padded, width), BF16),
             pltpu.VMEM((padded, width), BF16),
+            pltpu.VMEM((width, padded), BF16),
+            pltpu.VMEM((width, padded), BF16),
+            pltpu.VMEM((width, padded), BF16),
             pltpu.VMEM((count, width), BF16),
             pltpu.VMEM((count, width), BF16),
             pltpu.VMEM((count, padded), BF16),

time: 57.2 us -> 57.1 us (level)
  no operation moved by 1% of the time
where the time goes in v5:
time: 57.1 us; the launch traced here: 56.9 us
  Pallas kernels  55.4 us (97%)
  local copies, waits for them, and re-layouts  1.47 us (3%)
    pallas_call x1, Pallas kernels, dense(): pl.pallas_call(functools.partial(dense_kernel, blocks), out_shape=jax.Sha...  55.4 us
    unnamed x1, local copies, waits for them, and re-layouts  1.47 us

profile of v5, /device:TPU:0, one launch (start us, length us, event | category | flops | bytes accessed | tf_op | source)
XLA Modules:
  0.0 56.9 jit_solution(11587421776489808692)
XLA Ops:
  0.0 55.4 %shard_map.73 = bf16[16,2048]{1,0:T(8,128)(2,1)} custom-call(bf16[16,2048]{1,0:T(8,128)(2,1)} %tok_ref.1, bf16[16,2048]{1,0:T(8,128)(2,1)} %cot_ref.1, f32[4,16]{1,0:T(4,128)} %bitcast.2, s32[4,16]{1,0:T(4,128)} %bitcast.3, bf16[1,704,2048]{2,1,0:T(8,128)(2,1)} %wg_hbm.1, bf16[1,704,2048]{2,1,0:T(8,128)(2,1)} %wu_hbm.1, bf16[1,704,2048]{2,1,0:T(8,128)(2,1)} %wd_hbm.1), custom_call_target="tpu_custom_call" | custom-call | tf_op jit(solution)/shard_map/pallas_call | solution.py:271
  55.5 1.5 %copy.9 = bf16[16,2048]{1,0:T(8,128)(2,1)} copy(bf16[16,2048]{1,0:T(8,128)(2,1)} %shard_map.73) | data formatting | bytes 131072

commit v6 on v5

--- a/solution.py
+++ b/solution.py
@@ -127,16 +127,16 @@
         for r in range(4):
             cross[i, r].wait_recv()
 
-    count = 2 * CORES * 4 * tok_dev
+    count = CORES * 4 * tok_dev
 
     def expand(i):
-        gate_rows = rows[pl.ds(i, 2), :, :, :, pl.ds(2 * width, LANES)].reshape(count, LANES)
+        gate_rows = rows[i, :, :, :, pl.ds(2 * width, LANES)].reshape(count, LANES)
         lanes = lax.broadcasted_iota(jnp.int32, (count, LANES), 1)
         mine = (lanes % experts == expert) & (lanes < 3 * experts)
         gate = jnp.sum(jnp.where(mine, gate_rows.astype(F32), 0.0), axis=1, keepdims=True)
-        cot = rows[pl.ds(i, 2), :, :, :, pl.ds(width, width)].reshape(count, width)
+        cot = rows[i, :, :, :, pl.ds(width, width)].reshape(count, width)
         ys[...] = (gate * cot.astype(F32)).astype(BF16)
-        xs[...] = rows[pl.ds(i, 2), :, :, :, pl.ds(0, width)].reshape(count, width)
+        xs[...] = rows[i, :, :, :, pl.ds(0, width)].reshape(count, width)
 
     def turn(k):
         loads[k].wait()
@@ -169,13 +169,12 @@
             at = pl.ds(pl.multiple_of(which * half + n * step, step), step)
             value = jnp.dot(dgs[...], wg[:, at], preferred_element_type=F32)
             value += jnp.dot(dus[...], wu[:, at], preferred_element_type=F32)
-            part[pl.ds(i, 2), :, :, :, at] = value.astype(BF16).reshape(2, CORES, 4, tok_dev, step)
+            part[i, :, :, :, at] = value.astype(BF16).reshape(CORES, 4, tok_dev, step)
             return carry
 
         lax.fori_loop(0, 2, body, 0)
-        for k in (i + 1, i):
-            at = pl.ds(which * half, half)
-            sib[k, which] = send(part.at[k, 1, :, :, at], from_sib.at[k, :, :, at], sibling)
+        at = pl.ds(which * half, half)
+        sib[i, which] = send(part.at[i, 1, :, :, at], from_sib.at[i, :, :, at], sibling)
 
     sib, first_x, first_y, second_x, second_y, home = {}, {}, {}, {}, {}, {}
 
@@ -206,6 +205,13 @@
         plane[i, :, half:] = right.astype(BF16)
         if i:
             home[i] = send(plane.at[i], from_z.at[i - 1], at_z[i])
+
+    def products(i):
+        arrived(i)
+        expand(i)
+        forward()
+        back(i, 0)
+        back(i, 1)
 
     spread(0)
     for i in (1, 2, 3):
@@ -217,39 +223,33 @@
         relay(i - 1)
         turn(i)
     close(0)
+    products(0)
     along_z[3].wait_recv()
     spread(3)
     close(1)
     relay(2)
-    arrived(0)
-    arrived(1)
-    expand(0)
-    forward()
+    products(1)
+    close(2)
     relay(3)
-    close(2)
-    back(0, 0)
-    back(0, 1)
+    for which in (0, 1):
+        reduce_first(0, which)
+    products(2)
     close(3)
-    for i in (1, 0):
-        reduce_first(i, 0)
-        reduce_first(i, 1)
-    arrived(2)
-    arrived(3)
-    expand(2)
-    forward()
+    for which in (0, 1):
+        reduce_first(1, which)
+    reduce_second(0)
+    for which in (0, 1):
+        reduce_first(2, which)
+    products(3)
     reduce_second(1)
-    reduce_second(0)
-    back(2, 0)
-    reduce_third(1)
-    reduce_third(0)
-    back(2, 1)
+    reduce_second(2)
     for which in (0, 1):
         reduce_first(3, which)
-        reduce_first(2, which)
-    for i in (3, 2):
-        reduce_second(i)
-    for i in (3, 2):
+    for i in (1, 2):
         reduce_third(i)
+    reduce_second(3)
+    reduce_third(3)
+    reduce_third(0)
     total = plane[0].astype(F32)
     for i in (1, 2, 3):
         home[i].wait_recv()
@@ -263,7 +263,7 @@
     tok_dev, width = tokens.shape
     padded = -(-w_gate.shape[1] // TILE) * TILE
     blocks = lax.axis_size("hid") // EXP_DEV
-    count = 2 * CORES * 4 * tok_dev
+    count = CORES * 4 * tok_dev
     half = width // 2
     top = gates.shape[1]
     hbm = pl.BlockSpec(memory_space=pltpu.HBM)

time: 57.1 us -> 57 us (level)
  no operation moved by 1% of the time
where the time goes in v6:
time: 57 us; the launch traced here: 56.9 us
  Pallas kernels  55.4 us (97%)
  local copies, waits for them, and re-layouts  1.47 us (3%)
    pallas_call x1, Pallas kernels, dense(): pl.pallas_call(functools.partial(dense_kernel, blocks), out_shape=jax.Sha...  55.4 us
    unnamed x1, local copies, waits for them, and re-layouts  1.47 us

profile of v6, /device:TPU:0, one launch (start us, length us, event | category | flops | bytes accessed | tf_op | source)
XLA Modules:
  0.0 56.9 jit_solution(11694072395871350480)
XLA Ops:
  0.0 55.4 %shard_map.73 = bf16[16,2048]{1,0:T(8,128)(2,1)} custom-call(bf16[16,2048]{1,0:T(8,128)(2,1)} %tok_ref.1, bf16[16,2048]{1,0:T(8,128)(2,1)} %cot_ref.1, f32[4,16]{1,0:T(4,128)} %bitcast.2, s32[4,16]{1,0:T(4,128)} %bitcast.3, bf16[1,704,2048]{2,1,0:T(8,128)(2,1)} %wg_hbm.1, bf16[1,704,2048]{2,1,0:T(8,128)(2,1)} %wu_hbm.1, bf16[1,704,2048]{2,1,0:T(8,128)(2,1)} %wd_hbm.1), custom_call_target="tpu_custom_call" | custom-call | tf_op jit(solution)/shard_map/pallas_call | solution.py:271
  55.4 1.5 %copy.9 = bf16[16,2048]{1,0:T(8,128)(2,1)} copy(bf16[16,2048]{1,0:T(8,128)(2,1)} %shard_map.73) | data formatting | bytes 131072

commit v7 on v6

--- a/solution.py
+++ b/solution.py
@@ -56,7 +56,7 @@
     def device(zz, cc, yy, xx):
         return (zz * CORES + cc, yy * 2 + xx)
 
-    z_of = (z, z + 1 - 2 * (z % 2), (z + 2) % 4, 3 - z)
+    z_of = (z, (z + 2) % 4, 3 - z, z + 1 - 2 * (z % 2))
     at_x = device(z, c, y, 1 - x)
     at_y = device(z, c, 1 - y, x)
     sibling = device(z, 1 - c, y, x)
@@ -213,9 +213,10 @@
         back(i, 0)
         back(i, 1)
 
+    for i in (1, 2):
+        along_z[i] = send(rows.at[0, 0, 0], rows.at[i, 0, 0], at_z[i])
     spread(0)
-    for i in (1, 2, 3):
-        along_z[i] = send(rows.at[0, 0, 0], rows.at[i, 0, 0], at_z[i])
+    along_z[3] = send(rows.at[0, 0, 0], rows.at[3, 0, 0], at_z[3])
     turn(0)
     for i in (1, 2):
         along_z[i].wait_recv()

time: 57 us -> 58.7 us (1.030)
  Pallas kernels: 55.4 us -> 57.1 us
    pallas_call x1, Pallas kernels: 55.4 us -> 57.1 us  [dense(): pl.pallas_call(functools.partial(dense_kernel, blocks), out_shape=jax.Sha...]
where the time goes in v7:
time: 58.7 us; the launch traced here: 58.6 us
  Pallas kernels  57.1 us (97%)
  local copies, waits for them, and re-layouts  1.47 us (3%)
    pallas_call x1, Pallas kernels, dense(): pl.pallas_call(functools.partial(dense_kernel, blocks), out_shape=jax.Sha...  57.1 us
    unnamed x1, local copies, waits for them, and re-layouts  1.47 us

profile of v7, /device:TPU:0, one launch (start us, length us, event | category | flops | bytes accessed | tf_op | source)
XLA Modules:
  0.0 58.6 jit_solution(15289416675363530844)
XLA Ops:
  0.0 57.1 %shard_map.73 = bf16[16,2048]{1,0:T(8,128)(2,1)} custom-call(bf16[16,2048]{1,0:T(8,128)(2,1)} %tok_ref.1, bf16[16,2048]{1,0:T(8,128)(2,1)} %cot_ref.1, f32[4,16]{1,0:T(4,128)} %bitcast.2, s32[4,16]{1,0:T(4,128)} %bitcast.3, bf16[1,704,2048]{2,1,0:T(8,128)(2,1)} %wg_hbm.1, bf16[1,704,2048]{2,1,0:T(8,128)(2,1)} %wu_hbm.1, bf16[1,704,2048]{2,1,0:T(8,128)(2,1)} %wd_hbm.1), custom_call_target="tpu_custom_call" | custom-call | tf_op jit(solution)/shard_map/pallas_call | solution.py:272
  57.1 1.5 %copy.9 = bf16[16,2048]{1,0:T(8,128)(2,1)} copy(bf16[16,2048]{1,0:T(8,128)(2,1)} %shard_map.73) | data formatting | bytes 131072

commit v8 on v6

--- a/solution.py
+++ b/solution.py
@@ -240,13 +240,17 @@
     reduce_second(0)
     for which in (0, 1):
         reduce_first(2, which)
-    products(3)
     reduce_second(1)
+    arrived(3)
+    expand(3)
+    forward()
     reduce_second(2)
+    reduce_third(1)
+    back(3, 0)
+    back(3, 1)
     for which in (0, 1):
         reduce_first(3, which)
-    for i in (1, 2):
-        reduce_third(i)
+    reduce_third(2)
     reduce_second(3)
     reduce_third(3)
     reduce_third(0)

time: 57 us -> 59.5 us (1.044)
  Pallas kernels: 55.4 us -> 57.9 us
    pallas_call x1, Pallas kernels: 55.4 us -> 57.9 us  [dense(): pl.pallas_call(functools.partial(dense_kernel, blocks), out_shape=jax.Sha...]
where the time goes in v8:
time: 59.5 us; the launch traced here: 59.3 us
  Pallas kernels  57.9 us (97%)
  local copies, waits for them, and re-layouts  1.47 us (2%)
    pallas_call x1, Pallas kernels, dense(): pl.pallas_call(functools.partial(dense_kernel, blocks), out_shape=jax.Sha...  57.9 us
    unnamed x1, local copies, waits for them, and re-layouts  1.47 us

profile of v8, /device:TPU:0, one launch (start us, length us, event | category | flops | bytes accessed | tf_op | source)
XLA Modules:
  0.0 59.3 jit_solution(1796939387020643657)
XLA Ops:
  0.0 57.9 %shard_map.73 = bf16[16,2048]{1,0:T(8,128)(2,1)} custom-call(bf16[16,2048]{1,0:T(8,128)(2,1)} %tok_ref.1, bf16[16,2048]{1,0:T(8,128)(2,1)} %cot_ref.1, f32[4,16]{1,0:T(4,128)} %bitcast.2, s32[4,16]{1,0:T(4,128)} %bitcast.3, bf16[1,704,2048]{2,1,0:T(8,128)(2,1)} %wg_hbm.1, bf16[1,704,2048]{2,1,0:T(8,128)(2,1)} %wu_hbm.1, bf16[1,704,2048]{2,1,0:T(8,128)(2,1)} %wd_hbm.1), custom_call_target="tpu_custom_call" | custom-call | tf_op jit(solution)/shard_map/pallas_call | solution.py:275
  57.9 1.5 %copy.9 = bf16[16,2048]{1,0:T(8,128)(2,1)} copy(bf16[16,2048]{1,0:T(8,128)(2,1)} %shard_map.73) | data formatting | bytes 131072
